TPU v7x, 256 devices: a whole 4x4x8 slice. The times are simulated.
256 devices in a mesh: dp: 256 (over z, x, y, core).
Axes of the slice: x: 4, y: 4, z: 8, core: 2. Of those that a mesh axis runs over, the one named last changes fastest.
Arguments:
- img_feats: bfloat16 [131072, 1152], P('dp'), may hold values from -6 to 6
- txt_feats: bfloat16 [131072, 1152], P('dp'), may hold values from -6 to 6
- img_head: bfloat16 [1152, 1152], replicated, may hold values from -0.1875 to 0.1875
- txt_head: bfloat16 [1152, 1152], replicated, may hold values from -0.1875 to 0.1875
- log_temp: float32 [], replicated, may hold values from 1.5 to 2.5
- logit_bias: float32 [], replicated, may hold values from -6 to -2
- caption_row: int32 [131072], P('dp'), may hold values from 0 to 511, as said below
Outputs:
- head_grads: float32 [2304, 1152], P('dp')
Inputs may be any that keep to these rules, and one draw needn't show every extreme that they name: `caption_row`: each device's block of 512 entries is a permutation of 0 .. 511.
All inputs are finite; a program needn't handle non-finite values.
Results may differ from a plain program's by a relative error of at most 0.0023.
Values may be sent and summed in bfloat16 or wider, within the bound.
No kernel may reach another device: no remote copies, remote signals or barrier semaphores. Data moves between devices by JAX's collectives and lax.ppermute only.
A program may use at most 128 MiB of HBM per device.

v0:
```python
import jax
import jax.numpy as jnp
from jax import lax
from jax.sharding import PartitionSpec as P

ROUNDS = 2


def partner(value, axis, bit):
    mask = 2**bit
    pairs = [(source, source ^ mask) for source in range(lax.axis_size(axis))]
    return lax.ppermute(value, axis, pairs)


def embed(features, head):
    projected = jnp.dot(features, head, preferred_element_type=jnp.float32)
    scale = jnp.sqrt(jnp.sum(projected * projected, axis=-1, keepdims=True) + 1e-06)
    return (projected / scale, scale)


def tile_slope(left, right, label_sign, temper, offset):
    scores = temper * jnp.dot(left, right.T, preferred_element_type=jnp.float32) + offset
    margin = label_sign * scores
    return (-label_sign * jax.nn.sigmoid(-margin) * temper).astype(jnp.bfloat16)


def per_device(img_feats, txt_feats, img_head, txt_head, log_temp, logit_bias, caption_row):
    img_unit, img_scale = embed(img_feats, img_head)
    txt_unit, txt_scale = embed(txt_feats, txt_head)
    img_low = img_unit.astype(jnp.bfloat16)
    txt_low = txt_unit.astype(jnp.bfloat16)
    temper = jnp.exp(log_temp)
    block_rows = caption_row.shape[0]
    columns = jnp.arange(block_rows, dtype=jnp.int32)
    label_sign = jnp.where(columns[None, :] == caption_row[:, None], 1.0, -1.0).astype(jnp.float32)
    negative = jnp.float32(-1.0)
    slope = tile_slope(img_low, txt_low, label_sign, temper, logit_bias)
    img_grad = jnp.dot(slope, txt_low, preferred_element_type=jnp.float32)
    txt_grad = jnp.dot(slope.T, img_low, preferred_element_type=jnp.float32)
    levels = lax.axis_size("dp").bit_length() - 1
    for turn_index in range(ROUNDS):
        bit_number = levels - 1 - turn_index
        far_txt = partner(txt_low, "dp", bit_number)
        slope = tile_slope(img_low, far_txt, negative, temper, logit_bias)
        img_grad = img_grad + jnp.dot(slope, far_txt, preferred_element_type=jnp.float32)
        partial_value = jnp.dot(slope.T, img_low, preferred_element_type=jnp.float32)
        txt_grad = txt_grad + partner(partial_value, "dp", bit_number)
    img_dz = (
        (img_grad - img_unit * jnp.sum(img_unit * img_grad, axis=-1, keepdims=True)) / img_scale
    ).astype(jnp.bfloat16)
    txt_dz = (
        (txt_grad - txt_unit * jnp.sum(txt_unit * txt_grad, axis=-1, keepdims=True)) / txt_scale
    ).astype(jnp.bfloat16)
    width = img_feats.shape[1]
    entries = 2 * width * width
    stacked = jnp.concatenate(
        [
            jnp.dot(img_feats.T, img_dz, preferred_element_type=jnp.float32),
            jnp.dot(txt_feats.T, txt_dz, preferred_element_type=jnp.float32),
        ],
        axis=0,
    )
    my_rows = lax.psum_scatter(stacked, "dp", scatter_dimension=0, tiled=True)
    local_square = jnp.sum(my_rows * my_rows)
    square_total = lax.psum(local_square, "dp")
    spread = jnp.sqrt(square_total / entries + 1e-06)
    return my_rows / spread


def solution(mesh):
    return jax.shard_map(
        per_device,
        mesh=mesh,
        in_specs=(P("dp", None), P("dp", None), P(), P(), P(), P(), P("dp")),
        out_specs=P("dp", None),
        check_vma=False,
    )
```

profile of v0, /device:TPU:1, one launch (start us, length us, event | category | flops | bytes accessed | tf_op | source)
XLA Modules:
  0.0 715.1 jit_solution(4993454022888173378)
XLA Ops:
  6.5 1.7 copy-done
  8.3 3.2 multiply_reduce_fusion.2
  11.5 0.0 copy-start.4
  11.5 0.3 fusion.27
  11.8 1.1 copy-done.2
  12.9 7.7 %collective-permute-start = (bf16[512,1152]{1,0:T(8,128)(2,1)S(1)}, bf16[512,1152]{1,0:T(8,128)(2,1)}, u32[]{:S(2)}, u32[]{:S(2)}) collective-permute-start(bf16[512,1152]{1,0:T(8,128)(2,1)S(1)} %fusion.27), channel_id=1, source_target_pairs={{0,128},{1,129},{2,130},{3,131},{4,132},{5,133},{6,134},{7,135},{8... | collective-permute-start | bytes 3538952 | tf_op jit(solution)/shard_map/ppermute | solution.py:12
  20.7 1.2 collective-permute-start.1
  23.2 3.7 multiply_reduce_fusion.3
  26.9 0.3 fusion.26
  27.2 26.0 %collective-permute-done = bf16[512,1152]{1,0:T(8,128)(2,1)} collective-permute-done((bf16[512,1152]{1,0:T(8,128)(2,1)S(1)}, bf16[512,1152]{1,0:T(8,128)(2,1)}, u32[]{:S(2)}, u32[]{:S(2)}) %collective-permute-start) | collective-permute-done | bytes 1179680 | tf_op jit(solution)/shard_map/ppermute | solution.py:12
  53.2 2.3 fusion.17
  55.5 0.9 fusion.29
  56.3 6.8 collective-permute-start.2
  63.1 161.8 %collective-permute-done.1 = bf16[512,1152]{1,0:T(8,128)(2,1)} collective-permute-done((bf16[512,1152]{1,0:T(8,128)(2,1)S(1)}, bf16[512,1152]{1,0:T(8,128)(2,1)}, u32[]{:S(2)}, u32[]{:S(2)}) %collective-permute-start.1) | collective-permute-done | bytes 1179680 | tf_op jit(solution)/shard_map/ppermute | solution.py:12
  224.9 2.3 fusion.16
  227.2 0.0 copy-start.7
  227.2 0.9 fusion.30
  228.1 0.3 collective-permute-start.3
  228.4 1.2 fusion.21
  229.6 0.8 fusion.28
  230.4 2.1 convolution_add_fusion.2
  232.6 2.5 multiply_reduce_fusion.1
  235.1 4.4 convolution_bitcast_fusion.1
  239.5 93.2 %collective-permute-done.3 = f32[512,1152]{1,0:T(8,128)S(1)} collective-permute-done((f32[512,1152]{1,0:T(8,128)S(1)}, f32[512,1152]{1,0:T(8,128)S(1)}, u32[]{:S(2)}, u32[]{:S(2)}) %collective-permute-start.3) | collective-permute-done | bytes 2359328 | tf_op jit(solution)/shard_map/ppermute | solution.py:12
  332.7 1.3 multiply_reduce_fusion
  334.0 4.3 convolution_bitcast_fusion
  338.3 8.8 %pad_maximum_fusion = f32[2304,1152]{1,0:T(8,128)} fusion(f32[1152,1152]{1,0:T(8,128)} %convolution_bitcast_fusion, f32[1152,1152]{1,0:T(8,128)} %convolution_bitcast_fusion.1), kind=kLoop, calls=%fused_computation | loop fusion | flops 2654208 | bytes 21233664 | tf_op jit(solution)/shard_map/concatenate | solution.py:56
  347.1 0.0 all-reduce.3.cloned.1.call-update
  347.1 279.8 %all-reduce.3.cloned.1.call-done = f32[2304,1152]{1,0:T(8,128)} async-done(((f32[2304,1152]{1,0:T(8,128)}), f32[2304,1152]{1,0:T(8,128)}) %all-reduce.3.cloned.1.call-update) | async-done | bytes 10616848
  626.9 1.5 multiply_reduce_fusion.4
  628.4 77.6 %psum.7 = f32[]{:T(128)} all-reduce(f32[]{:T(128)} %multiply_reduce_fusion.4), channel_id=1, replica_groups=mesh['dp'=256] {'dp'}, use_global_device_ids=true, to_apply=%region_6.7 | all-reduce | flops 1 | bytes 8 | tf_op jit(solution)/shard_map/psum | solution.py:65
  706.7 1.6 dynamic-slice_divide_fusion
  (16 shorter events, 0.0 us)
Async XLA Ops:
  6.5 1.8 copy-start
  6.5 620.4 %all-reduce.3.cloned.1.call-start = ((), (), s32[]{:S(2)}) async-start(), calls=%async_computation | async-start | bytes 21233664
  11.5 1.4 copy-start.2
  11.5 11.7 %copy-start.4 = (bf16[512,1152]{1,0:T(8,128)(2,1)S(1)}, bf16[512,1152]{1,0:T(8,128)(2,1)}, u32[]{:S(2)}) copy-start(bf16[512,1152]{1,0:T(8,128)(2,1)} %param.7) | copy-start | bytes 3538948
  12.9 40.2 %collective-permute-start = (bf16[512,1152]{1,0:T(8,128)(2,1)S(1)}, bf16[512,1152]{1,0:T(8,128)(2,1)}, u32[]{:S(2)}, u32[]{:S(2)}) collective-permute-start(bf16[512,1152]{1,0:T(8,128)(2,1)S(1)} %fusion.27), channel_id=1, source_target_pairs={{0,128},{1,129},{2,130},{3,131},{4,132},{5,133},{6,134},{7,135},{8... | collective-permute-start | bytes 3538952 | tf_op jit(solution)/shard_map/ppermute | solution.py:12
  20.7 204.3 %collective-permute-start.1 = (bf16[512,1152]{1,0:T(8,128)(2,1)S(1)}, bf16[512,1152]{1,0:T(8,128)(2,1)}, u32[]{:S(2)}, u32[]{:S(2)}) collective-permute-start(bf16[512,1152]{1,0:T(8,128)(2,1)S(1)} %fusion.27), channel_id=1, source_target_pairs={{0,64},{1,65},{2,66},{3,67},{4,68},{5,69},{6,70},{7,71},{8,72},{9,... | collective-permute-start | bytes 3538952 | tf_op jit(solution)/shard_map/ppermute | solution.py:12
  56.3 183.1 %collective-permute-start.2 = (f32[512,1152]{1,0:T(8,128)S(1)}, f32[512,1152]{1,0:T(8,128)S(1)}, u32[]{:S(2)}, u32[]{:S(2)}) collective-permute-start(f32[512,1152]{1,0:T(8,128)S(1)} %fusion.29), channel_id=1, source_target_pairs={{0,128},{1,129},{2,130},{3,131},{4,132},{5,133},{6,134},{7,135},{8... | collective-permute-start | bytes 7077896 | tf_op jit(solution)/shard_map/ppermute | solution.py:12
  227.2 1.2 copy-start.7
  228.1 104.6 %collective-permute-start.3 = (f32[512,1152]{1,0:T(8,128)S(1)}, f32[512,1152]{1,0:T(8,128)S(1)}, u32[]{:S(2)}, u32[]{:S(2)}) collective-permute-start(f32[512,1152]{1,0:T(8,128)S(1)} %fusion.30), channel_id=1, source_target_pairs={{0,64},{1,65},{2,66},{3,67},{4,68},{5,69},{6,70},{7,71},{8,72},{9,... | collective-permute-start | bytes 7077896 | tf_op jit(solution)/shard_map/ppermute | solution.py:12
  232.6 2.5 copy-start.5
  235.1 97.6 %copy-start.3 = (f32[512,1152]{1,0:T(8,128)S(1)}, f32[512,1152]{1,0:T(8,128)}, u32[]{:S(2)}) copy-start(f32[512,1152]{1,0:T(8,128)} %copy-done.2) | copy-start | bytes 7077892
  239.5 94.5 %copy-start.6 = (bf16[512,1152]{1,0:T(8,128)(2,1)S(1)}, bf16[512,1152]{1,0:T(8,128)(2,1)}, u32[]{:S(2)}) copy-start(bf16[512,1152]{1,0:T(8,128)(2,1)} %param.8) | copy-start | bytes 3538948
  347.1 361.2 %copy-start.1 = (bf16[1152,1152]{1,0:T(8,128)(2,1)S(1)}, bf16[1152,1152]{1,0:T(8,128)(2,1)}, u32[]{:S(2)}) copy-start(bf16[1152,1152]{1,0:T(8,128)(2,1)} %param.10) | copy-start | bytes 7962628
Sparse Core Ops, SparseCore 0:
  347.2 279.6 all-reduce.2
where the time goes:
time: 716 us; the launch traced here: 715 us
  waiting for transfers between devices  561 us (78%)
  blocking collectives  77.6 us (11%)
  matrix products  29.9 us (4%)
  starting transfers between devices  16 us (2%)
  between operations  15.6 us (2%)
  other arithmetic  12.4 us (2%)
    ppermute x4, waiting for transfers between devices, partner(): return lax.ppermute(value, axis, pairs)  281 us
    unnamed x2, waiting for transfers between devices  280 us
    psum x1, blocking collectives, per_device(): square_total = lax.psum(local_square, 'dp')  77.6 us
    ppermute x4, starting transfers between devices, partner(): return lax.ppermute(value, axis, pairs)  16 us
  transfers between devices with their start and end apart: 5, of which 4 were waited for; matrix products, arithmetic and copies ran while one was open for 3% of the time, Pallas kernels for 0%

commit v1 on v0

v1 whole, which is shorter than its diff:
```python
import jax
import jax.numpy as jnp
from jax import lax
from jax.sharding import PartitionSpec as P

SPLIT = 640


def permute(value, target):
    pairs = [(source, target(source)) for source in range(lax.axis_size("dp"))]
    return lax.ppermute(value, "dp", pairs)


def sibling(value):
    return permute(value, lambda d: d ^ 1)


def groups(bit, count):
    mask = (2**count - 1) << bit
    bases = [d for d in range(lax.axis_size("dp")) if not d & mask]
    return [[base + (k << bit) for k in range(2**count)] for base in bases]


def embed(features, head):
    projected = jnp.dot(features, head, preferred_element_type=jnp.float32)
    scale = jnp.sqrt(jnp.sum(projected * projected, axis=-1, keepdims=True) + 1e-06)
    return (projected / scale, scale)


def tile_slope(left, right, label_sign, temper, offset):
    scores = temper * jnp.dot(left, right.T, preferred_element_type=jnp.float32) + offset
    margin = label_sign * scores
    return (-label_sign * jax.nn.sigmoid(-margin) * temper).astype(jnp.bfloat16)


def to_dz(grad, unit, scale):
    inner = jnp.sum(unit * grad, axis=-1, keepdims=True)
    norm = jnp.sqrt(jnp.sum(grad * grad, axis=-1, keepdims=True))
    dz = ((grad - unit * inner) / scale).astype(jnp.bfloat16)
    return dz, jnp.sum(norm / scale)


def dot(a, b):
    return jnp.dot(a, b, preferred_element_type=jnp.float32)


def exchange_sum(block, bit, power):
    rows = block.shape[1]
    if power is not None:
        mark = jnp.full((4, 16, block.shape[2]), power, jnp.float16)
        block = jnp.concatenate([(block * jnp.exp2(14.0 - power)).astype(jnp.float16), mark], axis=1)
    got = lax.all_to_all(block, "dp", 0, 0, axis_index_groups=groups(bit, 2), tiled=True)
    if power is not None:
        back = jnp.exp2(got[:, rows, 0].astype(jnp.float32) - 14.0)
        got = got[:, :rows].astype(jnp.float32) * back[:, None, None]
    return jnp.sum(got, axis=0)


def per_device(img_feats, txt_feats, img_head, txt_head, log_temp, logit_bias, caption_row):
    core = lax.axis_index("dp") & 1
    first = core == 0
    width = img_feats.shape[1]
    block_rows = caption_row.shape[0]

    far_img = permute(img_feats, lambda d: d ^ (192 if d & 1 else 64))
    far_txt = permute(txt_feats, lambda d: d ^ (64 if d & 1 else 192))
    p = jnp.where(first, img_feats, txt_feats)
    q = jnp.where(first, txt_feats, img_feats)
    p_head = jnp.where(first, img_head, txt_head)
    q_head = jnp.where(first, txt_head, img_head)
    sib_q = sibling(q)

    temper = jnp.exp(log_temp)
    index = jnp.arange(block_rows, dtype=jnp.int32)
    match = jnp.where(first, caption_row, index)[:, None] == jnp.where(first, index, caption_row)[None, :]
    label_sign = jnp.where(match, 1.0, -1.0).astype(jnp.float32)
    negative = jnp.float32(-1.0)

    p_unit, p_scale = embed(p, p_head)
    q_unit, q_scale = embed(q, q_head)
    p_low = p_unit.astype(jnp.bfloat16)
    q_low = q_unit.astype(jnp.bfloat16)
    slope = tile_slope(p_low, q_low, label_sign, temper, logit_bias)
    p_dz, p_bound = to_dz(dot(slope, q_low), p_unit, p_scale)
    q_grad = dot(slope.T, p_low)

    pf = jnp.where(first, far_img, far_txt)
    qf = jnp.where(first, far_txt, far_img)
    sib_qf = sibling(qf)
    pf_unit, pf_scale = embed(pf, p_head)
    qf_unit, qf_scale = embed(qf, q_head)
    pf_low = pf_unit.astype(jnp.bfloat16)
    qf_low = qf_unit.astype(jnp.bfloat16)
    slope_a = tile_slope(pf_low, q_low, negative, temper, logit_bias)
    slope_b = tile_slope(pf_low, qf_low, negative, temper, logit_bias)
    q_dz, q_bound = to_dz(q_grad + dot(slope_a.T, pf_low), q_unit, q_scale)
    qf_dz, qf_bound = to_dz(dot(slope_b.T, pf_low), qf_unit, qf_scale)
    sib_q_dz = sibling(q_dz)
    sib_qf_dz = sibling(qf_dz)
    sib_bound = sibling(jnp.full((8, 128), q_bound + qf_bound, jnp.float32))
    pf_dz, pf_bound = to_dz(dot(slope_a, q_low) + dot(slope_b, qf_low), pf_unit, pf_scale)

    bound = 6.1 * (p_bound + pf_bound + sib_bound[0, 0])
    power = jnp.ceil(jnp.log2(jnp.maximum(bound, 1e-18)))
    feats = jnp.concatenate([p, sib_q, pf, sib_qf], axis=0)
    dz = jnp.concatenate([p_dz, sib_q_dz, pf_dz, sib_qf_dz], axis=0)

    left = dot(feats.T, dz[:, :SPLIT])
    right = dot(feats.T, dz[:, SPLIT:])
    left = exchange_sum(left.reshape(4, 288, SPLIT), 3, power)
    right = right.reshape(4, 4, 72, width - SPLIT).transpose(1, 0, 2, 3).reshape(4, 288, width - SPLIT)
    right = exchange_sum(right, 1, power)
    left = exchange_sum(left.reshape(4, 72, SPLIT), 1, None)
    right = exchange_sum(right.reshape(4, 72, width - SPLIT), 3, None)
    part = jnp.concatenate([left, right], axis=1).reshape(8, 9, width)
    got = lax.all_to_all(part, "dp", 0, 0, axis_index_groups=groups(5, 3), tiled=True)
    total = jnp.sum(got, axis=0)

    def owner(d):
        z, x, y, s = d >> 5, d >> 3 & 3, d >> 1 & 3, d & 1
        return (4 * s + x) << 5 | y << 3 | (z >> 1) << 1 | z & 1

    rows = permute(total, owner)
    squares = lax.all_gather(jnp.full((8, 128), jnp.sum(total * total), jnp.float32), "dp", tiled=True)
    entries = 2 * width * width
    spread = jnp.sqrt(jnp.sum(squares) / (1024.0 * entries) + 1e-06)
    return rows / spread


def solution(mesh):
    return jax.shard_map(
        per_device,
        mesh=mesh,
        in_specs=(P("dp", None), P("dp", None), P(), P(), P(), P(), P("dp")),
        out_specs=P("dp", None),
        check_vma=False,
    )
```

time: 716 us -> 277 us (0.39)
  waiting for transfers between devices: 561 us -> 88.2 us
  starting transfers between devices: 16 us -> 41.7 us
  other arithmetic: 12.4 us -> 22.8 us
  between operations: 15.6 us -> 5.63 us
    unnamed x2 -> x0, waiting for transfers between devices: 280 us -> none
    ppermute x4 -> x8, waiting for transfers between devices: 281 us -> 38.1 us  [permute(): return lax.ppermute(value, 'dp', pairs)]
    psum x1 -> x0, blocking collectives: 77.6 us -> none  [per_device(): square_total = lax.psum(local_square, 'dp')]
    unnamed x0 -> x1, blocking collectives: none -> 74.9 us
    all_to_all x0 -> x5, waiting for transfers between devices: none -> 50.1 us  [the longest x4 37.5 us: exchange_sum(): lax.all_to_all(block, 'dp', 0, 0, axis_index_groups=groups(bit, 2), tiled...]
    all_to_all x0 -> x5, starting transfers between devices: none -> 21.6 us  [the longest x4 15.4 us: exchange_sum(): lax.all_to_all(block, 'dp', 0, 0, axis_index_groups=groups(bit, 2), tiled...]
    convert_element_type x2 -> x5, other arithmetic: 0.56 us -> 7.9 us  [the longest x4 7.43 us: to_dz(): dz = ((grad - unit * inner) / scale).astype(jnp.bfloat16)]
    ppermute x4 -> x8, starting transfers between devices: 16 us -> 20.1 us  [permute(): return lax.ppermute(value, 'dp', pairs)]
  transfers between devices with their start and end apart: 5 -> 13, of which waited for: 4 -> 7; matrix products, arithmetic and copies ran while one was open for 3% -> 21% of each run, Pallas kernels for 0% -> 0%
where the time goes in v1:
time: 277 us; the launch traced here: 276 us
  waiting for transfers between devices  88.2 us (32%)
  blocking collectives  74.9 us (27%)
  starting transfers between devices  41.7 us (15%)
  matrix products  36.3 us (13%)
  other arithmetic  22.8 us (8%)
  local copies, waits for them, and re-layouts  6.52 us (2%)
  between operations  5.63 us (2%)
    unnamed x1, blocking collectives  74.9 us
    ppermute x8, waiting for transfers between devices, permute(): return lax.ppermute(value, 'dp', pairs)  38.1 us
    all_to_all x4, waiting for transfers between devices, exchange_sum(): lax.all_to_all(block, 'dp', 0, 0, axis_index_groups=groups(bit, 2), tiled...  37.5 us
    dot_general x8, matrix products, dot(): return jnp.dot(a, b, preferred_element_type=jnp.float32)  21.4 us
    ppermute x8, starting transfers between devices, permute(): return lax.ppermute(value, 'dp', pairs)  20.1 us
    all_to_all x4, starting transfers between devices, exchange_sum(): lax.all_to_all(block, 'dp', 0, 0, axis_index_groups=groups(bit, 2), tiled...  15.4 us
    all_to_all x1, waiting for transfers between devices, per_device(): lax.all_to_all(part, 'dp', 0, 0, axis_index_groups=groups(5, 3), tiled=True)  12.6 us
    dot_general x4, matrix products, embed(): projected = jnp.dot(features, head, preferred_element_type=jnp.float32)  11.6 us
  transfers between devices with their start and end apart: 13, of which 7 were waited for; matrix products, arithmetic and copies ran while one was open for 21% of the time, Pallas kernels for 0%

profile of v1, /device:TPU:1, one launch (start us, length us, event | category | flops | bytes accessed | tf_op | source)
XLA Modules:
  0.0 276.0 jit_solution(8762927585042016163)
XLA Ops:
  0.0 6.8 %collective-permute-start.1 = (bf16[512,1152]{1,0:T(8,128)(2,1)}, bf16[512,1152]{1,0:T(8,128)(2,1)S(1)}, u32[]{:S(2)}, u32[]{:S(2)}) collective-permute-start(bf16[512,1152]{1,0:T(8,128)(2,1)} %param.7), channel_id=1, source_target_pairs={{0,64},{1,193},{2,66},{3,195},{4,68},{5,197},{6,70},{7,199},{8,72}... | collective-permute-start | bytes 3538952 | tf_op jit(solution)/shard_map/ppermute | solution.py:11
  8.0 2.9 %broadcast_select_fusion.5 = (bf16[512,1152]{1,0:T(8,128)(2,1)S(1)}, bf16[512,1152]{1,0:T(8,128)(2,1)}) fusion(bf16[512,1152]{1,0:T(8,128)(2,1)} %param.7, bf16[512,1152]{1,0:T(8,128)(2,1)} %param.8, pred[]{:T(512)S(6)} %eq.16), kind=kLoop, calls=%fused_computation.69 | loop fusion | flops 1179648 | bytes 4718593 | tf_op jit(solution)/shard_map/jit(_where)/select_n | solution.py:67
  13.5 4.2 %multiply_reduce_fusion.12 = (f32[512]{0:T(512)S(1)}, f32[512,1152]{1,0:T(8,128)S(1)}) fusion(bf16[512,1152]{1,0:T(8,128)(2,1)} %get-tuple-element.14, bf16[1152,1152]{1,0:T(8,128)(2,1)} %param.10, bf16[1152,1152]{1,0:T(8,128)(2,1)} %param.9, pred[]{:T(512)S(6)} %eq.16), kind=kOutput, calls=%fused_computation.27 | convolution fusion | flops 1361460736 | bytes 8849409 | tf_op jit(solution)/shard_map/dot_general | solution.py:25
  17.8 2.0 multiply_reduce_fusion.13
  19.9 35.6 %collective-permute-done.1 = bf16[512,1152]{1,0:T(8,128)(2,1)S(1)} collective-permute-done((bf16[512,1152]{1,0:T(8,128)(2,1)}, bf16[512,1152]{1,0:T(8,128)(2,1)S(1)}, u32[]{:S(2)}, u32[]{:S(2)}) %collective-permute-start.1) | collective-permute-done | bytes 1179680 | tf_op jit(solution)/shard_map/ppermute | solution.py:11
  55.5 2.5 collective-permute-done.2
  59.2 2.0 multiply_reduce_fusion.10
  63.0 2.9 %multiply_reduce_fusion.5 = (f32[512]{0:T(512)}, f32[512]{0:T(512)}, f32[512,1152]{1,0:T(8,128)}) fusion(f32[512,1152]{1,0:T(8,128)S(1)} %get-tuple-element.28, f32[512]{0:T(512)S(1)} %add_sqrt_fusion.3, bf16[512,512]{1,0:T(8,128)(2,1)S(1)} %fusion.30, bf16[512,1152]{1,0:T(8,128)(2,1)S(1)} %get-tuple-element.31), kind=kOutput, calls=%fused_computation.16 | convolution fusion | flops 606927872 | bytes 6428672 | tf_op jit(solution)/shard_map/dot_general | solution.py:44
  66.8 3.3 %multiply_reduce_fusion.8 = (f32[512]{0:T(512)S(1)}, f32[512,1152]{1,0:T(8,128)S(1)}) fusion(bf16[512,1152]{1,0:T(8,128)(2,1)} %get-tuple-element.15, bf16[1152,1152]{1,0:T(8,128)(2,1)S(1)} %copy-done.12, bf16[1152,1152]{1,0:T(8,128)(2,1)S(1)} %copy-done.13, pred[]{:T(512)S(6)} %eq.16), kind=kOutput, calls=%fused_computation.21 | convolution fusion | flops 1361460736 | bytes 8849409 | tf_op jit(solution)/shard_map/dot_general | solution.py:25
  72.3 1.3 multiply_reduce_fusion.3
  73.6 1.5 divide_convert_fusion.2
  77.8 3.2 %multiply_reduce_fusion.4 = (f32[512]{0:T(512)}, f32[512]{0:T(512)}, f32[512,1152]{1,0:T(8,128)}) fusion(f32[512,1152]{1,0:T(8,128)S(1)} %get-tuple-element.20, f32[512]{0:T(512)S(1)} %add_sqrt_fusion.1, f32[512,1152]{1,0:T(8,128)S(1)} %fusion.52, bf16[512,512]{1,0:T(8,128)(2,1)S(1)} %fusion.25, f32[512,1152]{1,0:T(8,128)S(1)} %get-tuple-element.22, ...), kind=kOutput, calls=%fused_computation.15 | convolution fusion | flops 608697344 | bytes 9969664 | tf_op jit(solution)/shard_map/dot_general | solution.py:44
  81.1 1.5 divide_convert_fusion
  86.2 3.0 %divide_convert_fusion.3 = bf16[512,1152]{1,0:T(8,128)(2,1)S(1)} fusion(f32[512,1152]{1,0:T(8,128)} %get-tuple-element.30, f32[512]{0:T(512)} %get-tuple-element.12, f32[512]{0:T(512)S(1)} %add_sqrt_fusion.3, f32[512,1152]{1,0:T(8,128)} %copy-done.2), kind=kLoop, calls=%fused_computation.25 | loop fusion | flops 2949120 | bytes 5902336 | tf_op jit(solution)/shard_map/convert_element_type | solution.py:39
  89.9 1.5 divide_convert_fusion.1
  95.3 5.4 %fusion.1 = f16[1152,512]{1,0:T(8,128)(2,1)S(1)} fusion(bf16[512,1152]{1,0:T(8,128)(2,1)} %collective-permute-done.5, bf16[512,1152]{1,0:T(8,128)(2,1)} %divide_convert_fusion.1, bf16[512,1152]{1,0:T(8,128)(2,1)} %collective-permute-done.4, bf16[512,1152]{1,0:T(8,128)(2,1)S(1)} %divide_convert_fusion.3, f32[]{:T(128)S(6)} %exp2.25, ...), kind=kOutput, calls=%fused_computation.7 | convolution fusion | flops 2444361728 | bytes 10616836 | tf_op jit(solution)/shard_map/dot_general | solution.py:44
  101.0 1.3 concatenate.18
  102.4 4.4 %all-to-all-start.2 = ((f16[4,304,512]{2,1,0:T(8,128)(2,1)}), f16[4,304,512]{2,1,0:T(8,128)(2,1)S(1)}, u32[]{:S(2)}, u32[]{:S(2)}) async-start(f16[4,304,512]{2,1,0:T(8,128)(2,1)} %concatenate.18), calls=%async_computation.2 | async-start | bytes 2490368 | tf_op jit(solution)/shard_map/all_to_all | solution.py:52
  106.7 3.0 %pad_maximum_fusion.1 = bf16[2048,1152]{1,0:T(8,128)(2,1)S(1)} fusion(bf16[512,1152]{1,0:T(8,128)(2,1)} %collective-permute-done.5, bf16[512,1152]{1,0:T(8,128)(2,1)} %divide_convert_fusion.1, bf16[512,1152]{1,0:T(8,128)(2,1)} %collective-permute-done.4, bf16[512,1152]{1,0:T(8,128)(2,1)S(1)} %copy-done.1), kind=kLoop, calls=%fused_computation.1 | loop fusion | flops 18874368 | bytes 9437184 | tf_op jit(solution)/shard_map/concatenate | solution.py:106
  109.8 5.6 %fusion = f16[1152,640]{1,0:T(8,128)(2,1)S(1)} fusion(bf16[2048,1152]{1,0:T(8,128)(2,1)S(1)} %pad_maximum_fusion.1, f32[]{:T(128)S(6)} %exp2.25, bf16[512,1152]{1,0:T(8,128)(2,1)} %collective-permute-done.3, bf16[512,1152]{1,0:T(8,128)(2,1)S(1)} %copy-done.7, bf16[512,1152]{1,0:T(8,128)(2,1)} %collective-permute-done, bf16[512,1152]{1,0:T(8,128)(2,1)S(1)} %copy-done.5), kind=kOutput, calls=%fused_computation.6 | convolution fusion | flops 3040247808 | bytes 8814596 | tf_op jit(solution)/shard_map/dot_general | solution.py:44
  115.4 1.5 concatenate.17
  116.9 6.4 %all-to-all-done.2 = f16[4,304,512]{2,1,0:T(8,128)(2,1)S(1)} async-done(((f16[4,304,512]{2,1,0:T(8,128)(2,1)}), f16[4,304,512]{2,1,0:T(8,128)(2,1)S(1)}, u32[]{:S(2)}, u32[]{:S(2)}) %all-to-all-start.2) | async-done | bytes 1245216 | tf_op jit(solution)/shard_map/all_to_all | solution.py:52
  123.2 4.0 %all-to-all-start = ((f16[4,304,640]{2,1,0:T(8,128)(2,1)}), f16[4,304,640]{2,1,0:T(8,128)(2,1)S(1)}, u32[]{:S(2)}, u32[]{:S(2)}) async-start(f16[4,304,640]{2,1,0:T(8,128)(2,1)} %concatenate.17), calls=%async_computation | async-start | bytes 3112960 | tf_op jit(solution)/shard_map/all_to_all | solution.py:52
  128.5 17.3 %all-to-all-done = f16[4,304,640]{2,1,0:T(8,128)(2,1)S(1)} async-done(((f16[4,304,640]{2,1,0:T(8,128)(2,1)}), f16[4,304,640]{2,1,0:T(8,128)(2,1)S(1)}, u32[]{:S(2)}, u32[]{:S(2)}) %all-to-all-start) | async-done | bytes 1556512 | tf_op jit(solution)/shard_map/all_to_all | solution.py:52
  145.9 3.5 %all-to-all-start.3 = ((f32[4,72,512]{2,1,0:T(8,128)}), f32[4,72,512]{2,1,0:T(8,128)S(1)}, u32[]{:S(2)}, u32[]{:S(2)}) async-start(f32[4,72,512]{2,1,0:T(8,128)} %bitcast.6), calls=%async_computation.3 | async-start | bytes 1179648 | tf_op jit(solution)/shard_map/all_to_all | solution.py:52
  150.8 5.8 %all-to-all-done.3 = f32[4,72,512]{2,1,0:T(8,128)S(1)} async-done(((f32[4,72,512]{2,1,0:T(8,128)}), f32[4,72,512]{2,1,0:T(8,128)S(1)}, u32[]{:S(2)}, u32[]{:S(2)}) %all-to-all-start.3) | async-done | bytes 589856 | tf_op jit(solution)/shard_map/all_to_all | solution.py:52
  156.6 3.5 %all-to-all-start.1 = ((f32[4,72,640]{2,1,0:T(8,128)}), f32[4,72,640]{2,1,0:T(8,128)S(1)}, u32[]{:S(2)}, u32[]{:S(2)}) async-start(f32[4,72,640]{2,1,0:T(8,128)} %bitcast.2), calls=%async_computation.1 | async-start | bytes 1474560 | tf_op jit(solution)/shard_map/all_to_all | solution.py:52
  160.1 8.0 %all-to-all-done.1 = f32[4,72,640]{2,1,0:T(8,128)S(1)} async-done(((f32[4,72,640]{2,1,0:T(8,128)}), f32[4,72,640]{2,1,0:T(8,128)S(1)}, u32[]{:S(2)}, u32[]{:S(2)}) %all-to-all-start.1) | async-done | bytes 737312 | tf_op jit(solution)/shard_map/all_to_all | solution.py:52
  169.1 6.3 %all-to-all-start.4 = ((f32[8,9,1152]{2,1,0:T(8,128)}), f32[8,9,1152]{2,1,0:T(8,128)S(1)}, u32[]{:S(2)}, u32[]{:S(2)}) async-start(f32[8,9,1152]{2,1,0:T(8,128)} %reshape.69), calls=%async_computation.4 | async-start | bytes 1179648 | tf_op jit(solution)/shard_map/all_to_all | solution.py:116
  175.4 12.6 %all-to-all-done.4 = f32[8,9,1152]{2,1,0:T(8,128)S(1)} async-done(((f32[8,9,1152]{2,1,0:T(8,128)}), f32[8,9,1152]{2,1,0:T(8,128)S(1)}, u32[]{:S(2)}, u32[]{:S(2)}) %all-to-all-start.4) | async-done | bytes 331808 | tf_op jit(solution)/shard_map/all_to_all | solution.py:116
  188.0 9.5 %collective-permute-start.7 = (f32[9,1152]{1,0:T(8,128)S(1)}, f32[9,1152]{1,0:T(8,128)S(1)}, u32[]{:S(2)}, u32[]{:S(2)}) collective-permute-start(f32[9,1152]{1,0:T(8,128)S(1)} %reduce_sum.227), channel_id=1, source_target_pairs={{0,0},{1,128},{2,8},{3,136},{4,16},{5,144},{6,24},{7,152},{8,32},{... | collective-permute-start | bytes 124424 | tf_op jit(solution)/shard_map/ppermute | solution.py:11
  198.9 74.9 %all-reduce.2 = f32[256]{0:T(256)S(1)} all-reduce(f32[256]{0:T(256)S(1)} %dynamic-update-slice), channel_id=2, replica_groups=mesh['dp'=256] {'dp'}, use_global_device_ids=true, to_apply=%add.2 | all-reduce | flops 256 | bytes 2048
  (74 shorter events, 23.1 us)
Async XLA Ops:
  0.0 55.5 %collective-permute-start.1 = (bf16[512,1152]{1,0:T(8,128)(2,1)}, bf16[512,1152]{1,0:T(8,128)(2,1)S(1)}, u32[]{:S(2)}, u32[]{:S(2)}) collective-permute-start(bf16[512,1152]{1,0:T(8,128)(2,1)} %param.7), channel_id=1, source_target_pairs={{0,64},{1,193},{2,66},{3,195},{4,68},{5,197},{6,70},{7,199},{8,72}... | collective-permute-start | bytes 3538952 | tf_op jit(solution)/shard_map/ppermute | solution.py:11
  6.9 51.1 %collective-permute-start.2 = (bf16[512,1152]{1,0:T(8,128)(2,1)}, bf16[512,1152]{1,0:T(8,128)(2,1)S(1)}, u32[]{:S(2)}, u32[]{:S(2)}) collective-permute-start(bf16[512,1152]{1,0:T(8,128)(2,1)} %param.8), channel_id=1, source_target_pairs={{0,192},{1,65},{2,194},{3,67},{4,196},{5,69},{6,198},{7,71},{8,200... | collective-permute-start | bytes 3538952 | tf_op jit(solution)/shard_map/ppermute | solution.py:11
  10.9 6.8 %copy-start.4 = (bf16[512,1152]{1,0:T(8,128)(2,1)}, bf16[512,1152]{1,0:T(8,128)(2,1)S(1)}, u32[]{:S(2)}) copy-start(bf16[512,1152]{1,0:T(8,128)(2,1)S(1)} %get-tuple-element.13) | copy-start | bytes 3538948
  10.9 84.4 %collective-permute-start = (bf16[512,1152]{1,0:T(8,128)(2,1)}, bf16[512,1152]{1,0:T(8,128)(2,1)}, u32[]{:S(2)}, u32[]{:S(2)}) collective-permute-start(bf16[512,1152]{1,0:T(8,128)(2,1)} %get-tuple-element.14), channel_id=1, source_target_pairs={{0,1},{1,0},{2,3},{3,2},{4,5},{5,4},{6,7},{7,6},{8,9},{9,8},{10,11... | collective-permute-start | bytes 3538952 | tf_op jit(solution)/shard_map/ppermute | solution.py:11
  13.5 4.3 %copy-start.12 = (bf16[1152,1152]{1,0:T(8,128)(2,1)S(1)}, bf16[1152,1152]{1,0:T(8,128)(2,1)}, u32[]{:S(2)}) copy-start(bf16[1152,1152]{1,0:T(8,128)(2,1)} %param.10) | copy-start | bytes 7962628
  13.5 4.3 %copy-start.13 = (bf16[1152,1152]{1,0:T(8,128)(2,1)S(1)}, bf16[1152,1152]{1,0:T(8,128)(2,1)}, u32[]{:S(2)}) copy-start(bf16[1152,1152]{1,0:T(8,128)(2,1)} %param.9) | copy-start | bytes 7962628
  17.8 2.1 copy-start.9
  19.8 46.0 %copy-start.2 = (f32[512,1152]{1,0:T(8,128)}, f32[512,1152]{1,0:T(8,128)S(1)}, u32[]{:S(2)}) copy-start(f32[512,1152]{1,0:T(8,128)S(1)} %get-tuple-element.28) | copy-start | bytes 7077892
  59.2 2.0 copy-start.6
  70.1 25.2 %collective-permute-start.3 = (bf16[512,1152]{1,0:T(8,128)(2,1)}, bf16[512,1152]{1,0:T(8,128)(2,1)}, u32[]{:S(2)}, u32[]{:S(2)}) collective-permute-start(bf16[512,1152]{1,0:T(8,128)(2,1)} %get-tuple-element.15), channel_id=1, source_target_pairs={{0,1},{1,0},{2,3},{3,2},{4,5},{5,4},{6,7},{7,6},{8,9},{9,8},{10,11... | collective-permute-start | bytes 3538952 | tf_op jit(solution)/shard_map/ppermute | solution.py:11
  75.1 20.2 %collective-permute-start.4 = (bf16[512,1152]{1,0:T(8,128)(2,1)}, bf16[512,1152]{1,0:T(8,128)(2,1)}, u32[]{:S(2)}, u32[]{:S(2)}) collective-permute-start(bf16[512,1152]{1,0:T(8,128)(2,1)} %divide_convert_fusion.2), channel_id=1, source_target_pairs={{0,1},{1,0},{2,3},{3,2},{4,5},{5,4},{6,7},{7,6},{8,9},{9,8},{10,11... | collective-permute-start | bytes 3538952 | tf_op jit(solution)/shard_map/ppermute | solution.py:11
  82.6 12.7 %collective-permute-start.5 = (bf16[512,1152]{1,0:T(8,128)(2,1)}, bf16[512,1152]{1,0:T(8,128)(2,1)}, u32[]{:S(2)}, u32[]{:S(2)}) collective-permute-start(bf16[512,1152]{1,0:T(8,128)(2,1)} %divide_convert_fusion), channel_id=1, source_target_pairs={{0,1},{1,0},{2,3},{3,2},{4,5},{5,4},{6,7},{7,6},{8,9},{9,8},{10,11... | collective-permute-start | bytes 3538952 | tf_op jit(solution)/shard_map/ppermute | solution.py:11
  85.7 7.6 %collective-permute-start.6 = (f32[8,128]{1,0:T(8,128)}, f32[8,128]{1,0:T(8,128)}, u32[]{:S(2)}, u32[]{:S(2)}) collective-permute-start(f32[8,128]{1,0:T(8,128)} %broadcast_in_dim.14), channel_id=1, source_target_pairs={{0,1},{1,0},{2,3},{3,2},{4,5},{5,4},{6,7},{7,6},{8,9},{9,8},{10,11... | collective-permute-start | bytes 12296 | tf_op jit(solution)/shard_map/ppermute | solution.py:11
  86.2 3.0 %copy-start.10 = (f32[512]{0:T(512)S(1)}, f32[512]{0:T(512)}, u32[]{:S(2)}) copy-start(f32[512]{0:T(512)} %get-tuple-element.11) | copy-start | bytes 6148
  86.2 3.7 %copy-start.3 = (f32[512,1152]{1,0:T(8,128)S(1)}, f32[512,1152]{1,0:T(8,128)}, u32[]{:S(2)}) copy-start(f32[512,1152]{1,0:T(8,128)} %get-tuple-element.26) | copy-start | bytes 7077892
  86.2 3.7 %copy-start.8 = (f32[512]{0:T(512)S(1)}, f32[512]{0:T(512)}, u32[]{:S(2)}) copy-start(f32[512]{0:T(512)} %get-tuple-element.10) | copy-start | bytes 6148
  89.2 6.1 %copy-start = (bf16[512,1152]{1,0:T(8,128)(2,1)}, bf16[512,1152]{1,0:T(8,128)(2,1)S(1)}, u32[]{:S(2)}) copy-start(bf16[512,1152]{1,0:T(8,128)(2,1)S(1)} %divide_convert_fusion.3) | copy-start | bytes 3538948
  89.9 1.5 copy-start.11
  101.0 5.7 %copy-start.1 = (bf16[512,1152]{1,0:T(8,128)(2,1)S(1)}, bf16[512,1152]{1,0:T(8,128)(2,1)}, u32[]{:S(2)}) copy-start(bf16[512,1152]{1,0:T(8,128)(2,1)} %copy-done) | copy-start | bytes 3538948
  102.4 20.9 %all-to-all-start.2 = ((f16[4,304,512]{2,1,0:T(8,128)(2,1)}), f16[4,304,512]{2,1,0:T(8,128)(2,1)S(1)}, u32[]{:S(2)}, u32[]{:S(2)}) async-start(f16[4,304,512]{2,1,0:T(8,128)(2,1)} %concatenate.18), calls=%async_computation.2 | async-start | bytes 2490368 | tf_op jit(solution)/shard_map/all_to_all | solution.py:52
  106.7 3.0 %copy-start.5 = (bf16[512,1152]{1,0:T(8,128)(2,1)S(1)}, bf16[512,1152]{1,0:T(8,128)(2,1)}, u32[]{:S(2)}) copy-start(bf16[512,1152]{1,0:T(8,128)(2,1)} %copy-done.4) | copy-start | bytes 3538948
  106.7 3.1 %copy-start.7 = (bf16[512,1152]{1,0:T(8,128)(2,1)S(1)}, bf16[512,1152]{1,0:T(8,128)(2,1)}, u32[]{:S(2)}) copy-start(bf16[512,1152]{1,0:T(8,128)(2,1)} %copy-done.6) | copy-start | bytes 3538948
  123.2 22.6 %all-to-all-start = ((f16[4,304,640]{2,1,0:T(8,128)(2,1)}), f16[4,304,640]{2,1,0:T(8,128)(2,1)S(1)}, u32[]{:S(2)}, u32[]{:S(2)}) async-start(f16[4,304,640]{2,1,0:T(8,128)(2,1)} %concatenate.17), calls=%async_computation | async-start | bytes 3112960 | tf_op jit(solution)/shard_map/all_to_all | solution.py:52
  145.9 10.7 %all-to-all-start.3 = ((f32[4,72,512]{2,1,0:T(8,128)}), f32[4,72,512]{2,1,0:T(8,128)S(1)}, u32[]{:S(2)}, u32[]{:S(2)}) async-start(f32[4,72,512]{2,1,0:T(8,128)} %bitcast.6), calls=%async_computation.3 | async-start | bytes 1179648 | tf_op jit(solution)/shard_map/all_to_all | solution.py:52
  156.6 11.5 %all-to-all-start.1 = ((f32[4,72,640]{2,1,0:T(8,128)}), f32[4,72,640]{2,1,0:T(8,128)S(1)}, u32[]{:S(2)}, u32[]{:S(2)}) async-start(f32[4,72,640]{2,1,0:T(8,128)} %bitcast.2), calls=%async_computation.1 | async-start | bytes 1474560 | tf_op jit(solution)/shard_map/all_to_all | solution.py:52
  169.1 18.9 %all-to-all-start.4 = ((f32[8,9,1152]{2,1,0:T(8,128)}), f32[8,9,1152]{2,1,0:T(8,128)S(1)}, u32[]{:S(2)}, u32[]{:S(2)}) async-start(f32[8,9,1152]{2,1,0:T(8,128)} %reshape.69), calls=%async_computation.4 | async-start | bytes 1179648 | tf_op jit(solution)/shard_map/all_to_all | solution.py:116
  188.0 87.4 %collective-permute-start.7 = (f32[9,1152]{1,0:T(8,128)S(1)}, f32[9,1152]{1,0:T(8,128)S(1)}, u32[]{:S(2)}, u32[]{:S(2)}) collective-permute-start(f32[9,1152]{1,0:T(8,128)S(1)} %reduce_sum.227), channel_id=1, source_target_pairs={{0,0},{1,128},{2,8},{3,136},{4,16},{5,144},{6,24},{7,152},{8,32},{... | collective-permute-start | bytes 124424 | tf_op jit(solution)/shard_map/ppermute | solution.py:11
